TPU v7x, 32 devices: a whole 2x2x4 slice. The times are simulated.
32 devices in a mesh: expert: 8 (over z, x), tensor: 4 (over y, core).
Axes of the slice: x: 2, y: 2, z: 4, core: 2. Of those that a mesh axis runs over, the one named last changes fastest.
Arguments:
- inputs: bfloat16 [8192, 1536], P('expert'), may hold values from -6 to 6
- routes: int32 [8192, 4], P('expert'), may hold values from 0 to 7, all different within a row; in each aligned block of 1024 rows (0 to 1023, 1024 to 2047, ...) at most 768 rows name the same one
- cotangent: bfloat16 [8192, 1536], P('expert'), may hold values from -6 to 6
- first_gain: float32 [1536], replicated, may hold values from 0.5 to 1.5
- second_gain: float32 [1536], replicated, may hold values from 0.5 to 1.5
- w_query: bfloat16 [1536, 1536], P(None, 'tensor'), may hold values from -0.15625 to 0.15625
- w_key: bfloat16 [1536, 256], replicated, may hold values from -0.15625 to 0.15625
- w_value: bfloat16 [1536, 256], replicated, may hold values from -0.15625 to 0.15625
- w_output: bfloat16 [1536, 1536], P('tensor'), may hold values from -0.47851562 to 0.47851562
- w_router: bfloat16 [1536, 8], replicated, may hold values from -0.076660156 to 0.076660156
- w_gate: bfloat16 [8, 1536, 768], P('expert', None, 'tensor'), may hold values from -0.15625 to 0.15625
- w_up: bfloat16 [8, 1536, 768], P('expert', None, 'tensor'), may hold values from -0.15625 to 0.15625
- w_down: bfloat16 [8, 768, 1536], P('expert', 'tensor'), may hold values from -3 to 3
Outputs:
- layer_out: bfloat16 [8192, 1536], P('expert')
- grad_inputs: bfloat16 [8192, 1536], P('expert')
- grad_first: float32 [1536], replicated
- grad_second: float32 [1536], replicated
- grad_query: float32 [1536, 1536], P(None, 'tensor')
- grad_key: float32 [1536, 256], replicated
- grad_value: float32 [1536, 256], replicated
- grad_output: float32 [1536, 1536], P('tensor')
- grad_router: float32 [1536, 8], replicated
- grad_gate: float32 [8, 1536, 768], P('expert', None, 'tensor')
- grad_up: float32 [8, 1536, 768], P('expert', None, 'tensor')
- grad_down: float32 [8, 768, 1536], P('expert', 'tensor')
Inputs may be any that keep to these rules, and one draw needn't show every extreme that they name: `routes`: each row names 4 different experts. Within the rows of one device (aligned blocks of 1024 rows) no expert is named by more than 768 rows, a bound that some block reaches.
All inputs are finite; a program needn't handle non-finite values.
Results may differ from a plain program's by a relative error of at most 0.019.
Values may be sent and summed in bfloat16 or wider, within the bound.
A program may use at most 320 MiB of HBM per device.

v0:
```python
import functools

import jax
import jax.numpy as jnp
import numpy as np
from jax import lax
from jax.experimental import pallas as pl
from jax.experimental.pallas import tpu as pltpu
from jax.sharding import PartitionSpec as P

HEADS = 12
KV = 2
HD = 128
EPSILON = 1e-06
ROPE_BASE = 10000.0
NEGATIVE = -1e30
F32 = jnp.float32
BF16 = jnp.bfloat16


def dot(left, right, left_dim, right_dim):
    return lax.dot_general(
        left, right, (((left_dim,), (right_dim,)), ((), ())), preferred_element_type=F32
    )


def rms_norm(values, gain):
    inverse = lax.rsqrt(jnp.mean(values * values, axis=-1, keepdims=True) + EPSILON)
    normed = values * inverse
    return normed * gain, normed, inverse


def norm_backward(upstream, normed, inverse, gain):
    scaled = upstream * gain
    through = inverse * (scaled - normed * jnp.mean(scaled * normed, axis=-1, keepdims=True))
    return through, jnp.sum(upstream * normed, axis=0)


def rotary_tables(length):
    frequency = np.float32(ROPE_BASE) ** (-np.arange(HD // 2, dtype=np.float32) * np.float32(2.0 / HD))
    angles = np.arange(length, dtype=np.float32)[:, None] * frequency.astype(np.float32)[None]
    cos, sin = np.cos(angles), np.sin(angles)
    return np.concatenate([cos, cos], 1), np.concatenate([-sin, sin], 1)


def turned(values, cos, sin, back=False):
    other = pltpu.roll(values, HD // 2, 1) * sin
    return values * cos - other if back else values * cos + other


class Links:
    def __init__(self, experts, tensors):
        self.experts, self.tensors = experts, tensors
        self.line = experts // 2
        self.tensor = lax.axis_index("tensor")
        expert = lax.axis_index("expert")
        self.place, self.side = expert // 2, expert % 2

    def over_tensor(self, values, bit):
        return lax.ppermute(values, "tensor", [(i, i ^ bit) for i in range(self.tensors)])

    def over_expert(self, values, bit):
        return lax.ppermute(values, "expert", [(i, i ^ bit) for i in range(self.experts)])

    def over_pair(self, values):
        return self.over_expert(values, 1)

    def relative(self, values):
        rows = values.shape[0] // 4
        return jnp.concatenate(
            [
                lax.dynamic_slice_in_dim(values, (self.tensor ^ r) * rows, rows, 0)
                for r in (0, 2, 1, 3)
            ],
            0,
        )

    def absolute(self, values):
        rows = values.shape[0] // 4
        place = jnp.asarray([0, 2, 1, 3], jnp.int32)
        return jnp.concatenate(
            [
                lax.dynamic_slice_in_dim(values, place[self.tensor ^ q] * rows, rows, 0)
                for q in range(4)
            ],
            0,
        )

    def gather(self, quarter):
        both = jnp.concatenate([quarter, self.over_tensor(quarter, 2)], 0)
        return jnp.concatenate([both, self.over_tensor(both, 1)], 0)


def nearest_first(line):
    tables = []
    for place in range(line):
        offsets = [p - place for p in range(line) if p != place]
        tables.append(sorted(offsets, key=lambda o: (abs(o), -o)))
    return tables


def expert_kernel(count, hidden, split, prior, *refs):
    names, tokens, grads, gates = refs[:4]
    weights, refs = refs[4 : 4 + count], refs[4 + count :]
    if prior:
        before, refs = refs[0], refs[1:]
    outs, (gated_out, grad_pre_out, rows_out) = refs[: 2 if split else 1], refs[2 if split else 1 :]
    tile, grad_tile = tokens[...], grads[...]
    total = before[...].astype(F32) if prior else None
    for slot in range(count):
        weight = weights[slot]
        pre = dot(weight[: 2 * hidden, :], tile, 1, 1)
        back = dot(weight[2 * hidden :, :], grad_tile, 1, 1)
        gate = gates[pl.ds(names[slot], 1), :]
        gate_pre, up_pre = pre[:hidden], pre[hidden:]
        sigmoid = jax.nn.sigmoid(gate_pre)
        activated = gate_pre * sigmoid
        hid = (activated * up_pre).astype(BF16).astype(F32)
        rows_out[slot : slot + 1, :] = jnp.sum(hid * back, axis=0, keepdims=True)
        gated_out[slot * hidden : (slot + 1) * hidden, :] = (hid * gate).astype(BF16)
        grad_hidden = back * gate
        grad_pre = jnp.concatenate(
            [
                (grad_hidden * up_pre * (sigmoid * (1.0 + gate_pre * (1.0 - sigmoid)))).astype(BF16),
                (grad_hidden * activated).astype(BF16),
            ],
            0,
        )
        grad_pre_out[2 * slot * hidden : 2 * (slot + 1) * hidden, :] = grad_pre
        part = dot(grad_pre, weight[: 2 * hidden, :], 0, 0)
        total = part if total is None else total + part
    if split:
        for step in range(2):

            @pl.when(pl.program_id(0) == step)
            def _(step=step):
                outs[step][...] = total.astype(BF16)
    else:
        outs[0][...] = total.astype(BF16)


def expert_pass(tokens, grads, gates, names, weights, before=None, split=False):
    count, length, width = len(weights), tokens.shape[0], tokens.shape[1]
    hidden = weights[0].shape[0] // 3
    tile = length // 2
    token_spec = pl.BlockSpec((tile, width), lambda i, *_: (i, 0))
    half_spec = pl.BlockSpec((tile, width), lambda i, *_: (0, 0))

    def column_spec(rows):
        return pl.BlockSpec((rows, tile), lambda i, *_: (0, i))

    weight_spec = pl.BlockSpec((3 * hidden, width), lambda i, *_: (0, 0))
    token_shape = in_hbm((length, width), BF16)
    half_shape = in_hbm((tile, width), BF16)
    columns = [(count * hidden, BF16), (2 * count * hidden, BF16), (count, F32)]
    return pl.pallas_call(
        functools.partial(expert_kernel, count, hidden, split, before is not None),
        grid_spec=pltpu.PrefetchScalarGridSpec(
            num_scalar_prefetch=1,
            grid=(2,),
            in_specs=[token_spec, token_spec, column_spec(gates.shape[0])]
            + [weight_spec] * count
            + [token_spec] * (before is not None),
            out_specs=([half_spec] * 2 if split else [token_spec]) + [column_spec(r) for r, _ in columns],
        ),
        out_shape=([half_shape] * 2 if split else [token_shape])
        + [in_hbm((r, length), t) for r, t in columns],
        compiler_params=pltpu.CompilerParams(vmem_limit_bytes=48 * 2**20),
        cost_estimate=pl.CostEstimate(
            flops=2 * count * length * width * hidden * 5,
            bytes_accessed=(4 * length + 3 * hidden * count) * width * 2,
            transcendentals=0,
        ),
    )(names, *in_place([tokens, grads, gates, *weights] + ([before] if before is not None else [])))


def last_expert_kernel(hidden, weight, *refs):
    step = pl.program_id(0)
    weight_grad, total_grad = refs[-2:]

    @pl.when(step == 0)
    def _():
        total_grad[...] = jnp.zeros(total_grad.shape, F32)

    for side in range(2):
        tokens, grads, gate, before = refs[4 * side : 4 * side + 4]
        kept, sent, gated_out, row_out = refs[8 + 4 * side : 12 + 4 * side]

        @pl.when(step // 2 == side)
        def _(tokens=tokens, grads=grads, gate=gate, before=before, kept=kept, sent=sent, side=side,
              gated_out=gated_out, row_out=row_out):
            row, gated, grad_pre = hidden_units(weight, tokens[...], grads[...], gate[0:1, :], hidden)
            row_out[...] = row
            gated_out[...] = gated
            total_grad[: 2 * hidden, :] += dot(grad_pre, tokens[...], 1, 0)
            total_grad[2 * hidden :, :] += dot(gated, grads[...], 1, 0)
            total = (before[...].astype(F32) + dot(grad_pre, weight[: 2 * hidden, :], 0, 0)).astype(BF16)

            @pl.when(step % 2 == 0)
            def _():
                kept[...] = total

            @pl.when(step % 2 == 1)
            def _():
                sent[...] = total

    @pl.when(step == 3)
    def _():
        weight_grad[...] = total_grad[...].astype(BF16)


def last_expert(hidden, weight, pair, own):
    length, width = pair[0].shape
    tile = length // 2

    def specs(at):
        token = pl.BlockSpec((tile, width), lambda i: (at(i), 0))
        half = pl.BlockSpec((tile, width), lambda i: (0, 0))

        def column(rows):
            return pl.BlockSpec((rows, tile), lambda i: (0, at(i)))

        return [token, token, column(8), token], [half, half, column(hidden), column(1)]

    pair_ins, pair_outs = specs(lambda i: jnp.minimum(i, 1))
    own_ins, own_outs = specs(lambda i: jnp.maximum(i - 2, 0))
    shapes = [
        in_hbm((tile, width), BF16),
        in_hbm((tile, width), BF16),
        in_hbm((hidden, length), BF16),
        in_hbm((1, length), F32),
    ]
    whole = pl.BlockSpec((3 * hidden, width), lambda i: (0, 0))
    outs = pl.pallas_call(
        functools.partial(last_expert_kernel, hidden),
        grid=(4,),
        in_specs=[whole] + pair_ins + own_ins,
        out_specs=pair_outs + own_outs + [whole],
        out_shape=shapes * 2 + [in_hbm((3 * hidden, width), BF16)],
        scratch_shapes=[pltpu.VMEM((3 * hidden, width), F32)],
        compiler_params=pltpu.CompilerParams(vmem_limit_bytes=60 * 2**20),
        cost_estimate=pl.CostEstimate(
            flops=4 * length * width * hidden * 8,
            bytes_accessed=(8 * length + 3 * hidden) * width * 2,
            transcendentals=0,
        ),
    )(*in_place([weight, *pair, *own]))
    return outs[:4], outs[4:8], outs[8]


def weight_grad_kernel(grad_pre_own, grad_pre_pair, gated_own, gated_pair, own, pair, grad_own, grad_pair, out):
    rows = grad_pre_own.shape[0]
    out[:rows, :] = (
        dot(grad_pre_own[...], own[...], 1, 0) + dot(grad_pre_pair[...], pair[...], 1, 0)
    ).astype(out.dtype)
    out[rows:, :] = (
        dot(gated_own[...], grad_own[...], 1, 0) + dot(gated_pair[...], grad_pair[...], 1, 0)
    ).astype(out.dtype)


def weight_grad(slot, hidden, grad_pre, gated, tokens, grads, kept_as):
    length, width = tokens[0].shape
    tile = width // 3
    pre_spec = pl.BlockSpec((2 * hidden, length), lambda i: (slot, 0))
    gated_spec = pl.BlockSpec((hidden, length), lambda i: (slot, 0))
    token_spec = pl.BlockSpec((length, tile), lambda i: (0, i))
    return pl.pallas_call(
        weight_grad_kernel,
        grid=(3,),
        in_specs=[pre_spec] * 2 + [gated_spec] * 2 + [token_spec] * 4,
        out_specs=pl.BlockSpec((3 * hidden, tile), lambda i: (0, i)),
        out_shape=jax.ShapeDtypeStruct((3 * hidden, width), kept_as),
        compiler_params=pltpu.CompilerParams(vmem_limit_bytes=32 * 2**20),
        cost_estimate=pl.CostEstimate(
            flops=2 * 2 * length * width * hidden * 3,
            bytes_accessed=(4 * length + 6 * hidden) * width * 2,
            transcendentals=0,
        ),
    )(*grad_pre, *gated, *tokens, *grads)


MESH = pl.DeviceIdType.MESH


class Copies:
    def __init__(self, tensors, send, recv):
        self.send, self.recv, self.started, self.drained = send, recv, [], []
        expert, tensor = lax.axis_index("expert"), lax.axis_index("tensor")
        self.core = (expert, tensor + 1 - 2 * (tensor % 2))
        self.far = (expert, (tensor + tensors // 2) % tensors)
        self.mate = (expert + 1 - 2 * (expert % 2), tensor)

    def across(self, bit):
        expert, tensor = lax.axis_index("expert"), lax.axis_index("tensor")
        return (expert + bit - 2 * bit * (expert // bit % 2), tensor)

    def greet(self, partners, line=0):
        barrier = pltpu.get_barrier_semaphore()
        for partner in partners:
            pl.semaphore_signal(barrier, inc=1, device_id=partner, device_id_type=MESH)
        count = len(partners)
        if line:
            expert, tensor = lax.axis_index("expert"), lax.axis_index("tensor")
            position = expert // 2
            for step, there in ((2, position < line - 1), (-2, position > 0)):

                @pl.when(there)
                def _(step=step):
                    device = (expert + step, tensor)
                    pl.semaphore_signal(barrier, inc=1, device_id=device, device_id_type=MESH)

            count = count + 1 - (position + 1) // line + (position + line - 1) // line
        pl.semaphore_wait(barrier, count)

    def start(self, source, target, device):
        place = len(self.started)
        copy = pltpu.make_async_remote_copy(
            src_ref=source,
            dst_ref=target,
            send_sem=self.send.at[place],
            recv_sem=self.recv.at[place],
            device_id=device,
            device_id_type=MESH,
        )
        copy.start()
        self.started.append(copy)
        return copy

    def along(self, source, target, step, sends, receives):
        device = (lax.axis_index("expert") + 2 * step, lax.axis_index("tensor"))
        return self.over_when(source, target, device, sends, receives)

    def over_when(self, source, target, device, sends, receives=None):
        place = len(self.started)
        copy = pltpu.make_async_remote_copy(
            src_ref=source,
            dst_ref=target,
            send_sem=self.send.at[place],
            recv_sem=self.recv.at[place],
            device_id=device,
            device_id_type=MESH,
        )
        pl.when(sends)(lambda: copy.start())
        self.started.append(When(copy, sends, sends if receives is None else receives))
        return self.started[-1]

    def drain(self, copy):
        copy.wait_send()
        self.drained.append(copy)

    def finish(self):
        for copy in self.started:
            if all(copy is not done for done in self.drained):
                copy.wait_send()


class Moves:
    def __init__(self, semaphores):
        self.semaphores, self.count, self.open = semaphores, 0, []

    def start(self, *pairs):
        for source, target in pairs:
            copy = pltpu.make_async_copy(source, target, self.semaphores.at[self.count])
            copy.start()
            self.count += 1
            self.open.append(copy)

    def wait(self):
        for copy in self.open:
            copy.wait()
        self.open = []


def buffers_of(arrays):
    return [pltpu.VMEM(a.shape, a.dtype) for a in arrays]


class When:
    def __init__(self, copy, sends, receives):
        self.copy, self.sends, self.receives = copy, sends, receives

    def wait_send(self):
        pl.when(self.sends)(lambda: self.copy.wait_send())

    def wait_recv(self):
        pl.when(self.receives)(lambda: self.copy.wait_recv())


def sum_quarter(copies, part, sent, got, crossing, crossed, beside=None):
    rows = crossing.shape[0]
    sent[rows:, :] = part(3).astype(BF16)
    last = copies.start(sent.at[pl.ds(rows, rows)], got.at[pl.ds(rows, rows)], copies.core)
    sent[:rows, :] = part(2).astype(BF16)
    first = copies.start(sent.at[pl.ds(0, rows)], got.at[pl.ds(0, rows)], copies.core)
    other = part(1)
    last.wait_recv()
    crossing[...] = (other + got[rows:, :].astype(F32)).astype(BF16)
    far = copies.start(crossing, crossed, copies.far)
    if beside is not None:
        beside()
    mine = part(0)
    first.wait_recv()
    mine = mine + got[:rows, :].astype(F32)
    far.wait_recv()
    return mine + crossed[...].astype(F32)


def gather_quarters(copies, whole, rows, fill=None):
    far = copies.start(whole.at[pl.ds(0, rows)], whole.at[pl.ds(rows, rows)], copies.far)
    first = copies.start(whole.at[pl.ds(0, rows)], whole.at[pl.ds(2 * rows, rows)], copies.core)
    if fill is not None:
        fill()
    far.wait_recv()
    last = copies.start(whole.at[pl.ds(rows, rows)], whole.at[pl.ds(3 * rows, rows)], copies.core)
    first.wait_recv()
    last.wait_recv()


def quarter_at(place):
    tensor = lax.axis_index("tensor")
    return (tensor % 2 + place // 2) % 2 + 2 * ((tensor // 2 + place % 2) % 2)


def place_of(quarter):
    tensor = lax.axis_index("tensor")
    return 2 * ((tensor % 2 + quarter % 2) % 2) + (tensor // 2 + quarter // 2) % 2


def masked_scores(query, keys, start, scale):
    scores = dot(query, keys, 1, 1) * scale
    rows = lax.broadcasted_iota(jnp.int32, scores.shape, 0) + start
    cols = lax.broadcasted_iota(jnp.int32, scores.shape, 1)
    return jnp.where(cols <= rows, scores, NEGATIVE)


def kv_columns(heads):
    head = lax.axis_index("tensor") * heads // (HEADS // KV)
    return pl.ds(pl.multiple_of(head * HD, HD), HD)


def attend_kernel(tensors, line, heads, *refs):
    refs = list(refs)
    ins_there = [refs.pop(0) for _ in range(9)]
    own_weights = [refs.pop(0) for _ in range(3 if line else 0)]
    outs_there = [refs.pop(0) for _ in range(10)]
    arrived = refs.pop(0) if line else None
    ins, outs = [refs.pop(0) for _ in range(9)], [refs.pop(0) for _ in range(10)]
    stream, gain, w_query, w_key, w_value, cos, sin, grad, routes = ins
    attn_in, query, key, value, context, logsum, grad_rel, grad_pair, routes_own, routes_pair = outs
    local, send, recv = refs
    moves = Moves(local)
    moves.start(*zip(ins_there, ins))
    copies = Copies(tensors, send, recv)
    expert = lax.axis_index("expert")
    position = expert // 2
    copies.greet([copies.core, copies.mate], line)
    length = stream.shape[0]
    rows = length // 4
    if line:
        lines = []
        for index, weight in enumerate(own_weights):
            at = pl.ds(index * weight.shape[0], weight.shape[0])
            there = arrived.at[1 - (position + 2) // line, at]
            lines.append(copies.along(weight, there, 1, position < line - 1, position > 0))
            lines.append(copies.along(weight, arrived.at[0, at], -1, position > 0, position < line - 1))
    moves.wait()
    mates = []
    for place in range(4):
        at = pl.ds(place * rows, rows)
        grad_rel[at, :] = grad[pl.ds(pl.multiple_of(quarter_at(place) * rows, rows), rows), :]
        if place < 2:
            mates.append(copies.start(grad_rel.at[at], grad_pair.at[at], copies.mate))
    routes_own[...] = jnp.zeros(routes_own.shape, jnp.int32)
    for place in range(4):
        source = pl.ds(pl.multiple_of(quarter_at(place) * rows, rows), rows)
        routes_own[: routes.shape[0], place * rows : (place + 1) * rows] = routes[:, source]
    routes_copy = copies.start(routes_own, routes_pair, copies.mate)
    kv_at = kv_columns(heads)
    for tile in range(4):
        at = slice(tile * rows, (tile + 1) * rows)
        normed = rms_norm(stream[at, :].astype(F32), gain[...])[0].astype(BF16)
        attn_in[at, :] = normed
        proj = dot(normed, w_query[...], 1, 0)
        for head in range(heads):
            columns = slice(head * HD, (head + 1) * HD)
            query[at, columns] = turned(proj[:, columns], cos[at, :], sin[at, :]).astype(BF16)
        key[at, :] = turned(dot(normed, w_key[:, kv_at], 1, 0), cos[at, :], sin[at, :]).astype(BF16)
        value[at, :] = dot(normed, w_value[:, kv_at], 1, 0).astype(BF16)
    for tile in range(4):
        at, seen = slice(tile * rows, (tile + 1) * rows), (tile + 1) * rows
        to = pl.ds(pl.multiple_of(place_of(tile) * rows, rows), rows)
        for head in range(heads):
            columns = slice(head * HD, (head + 1) * HD)
            scores = masked_scores(query[at, columns], key[:seen, :], tile * rows, HD**-0.5)
            peak = jnp.max(scores, axis=-1, keepdims=True)
            exponent = jnp.exp(scores - peak)
            total = jnp.sum(exponent, axis=-1, keepdims=True)
            prob = (exponent / total).astype(BF16)
            context[to, columns] = dot(prob, value[:seen, :], 1, 0).astype(BF16)
            logsum[at, head : head + 1] = peak + jnp.log(total)
    pair_outs = (grad_pair, routes_pair)
    moves.start(*[pair for pair in zip(outs, outs_there) if all(pair[0] is not out for out in pair_outs)])
    cores = []
    for place in range(2):
        mates[place].wait_recv()
        source = grad_pair.at[pl.ds(place * rows, rows)]
        cores.append(copies.start(source, grad_pair.at[pl.ds((2 + place) * rows, rows)], copies.core))
    routes_copy.wait_recv()
    for copy in cores:
        copy.wait_recv()
    moves.start((grad_pair, outs_there[7]), (routes_pair, outs_there[9]))
    if line:
        for copy in lines:
            copy.wait_recv()
    moves.wait()
    copies.finish()


def anywhere():
    return pl.BlockSpec(memory_space=pl.ANY)


def attend(tensors, line, stream, gain, w_query, w_key, w_value, cos, sin, grad, routes, own_weights):
    length, width = stream.shape
    heads = w_query.shape[1] // HD
    outs = [
        ((length, width), BF16),
        ((length, heads * HD), BF16),
        ((length, HD), BF16),
        ((length, HD), BF16),
        ((length, heads * HD), BF16),
        ((length, HD), F32),
        ((length, width), BF16),
        ((length, width), BF16),
        ((8, length), routes.dtype),
        ((8, length), routes.dtype),
    ]
    operands = in_place([stream, gain, w_query, w_key, w_value, cos, sin, grad, routes])
    return pl.pallas_call(
        functools.partial(attend_kernel, tensors, line, heads),
        out_shape=[in_hbm(*out) for out in outs]
        + ([in_hbm((2, sum(w.shape[0] for w in own_weights), width), BF16)] if line else []),
        in_specs=[anywhere()] * (12 if line else 9),
        out_specs=[anywhere()] * (10 + bool(line)),
        scratch_shapes=buffers_of(operands)
        + [pltpu.VMEM(*out) for out in outs]
        + [
            pltpu.SemaphoreType.DMA((19,)),
            pltpu.SemaphoreType.DMA((12,)),
            pltpu.SemaphoreType.DMA((12,)),
        ],
        compiler_params=pltpu.CompilerParams(
            collective_id=4, has_side_effects=True, vmem_limit_bytes=48 * 2**20
        ),
        cost_estimate=pl.CostEstimate(flops=4 * 10**10, bytes_accessed=10**7, transcendentals=0),
    )(*operands, *(in_place(own_weights) if line else []))


def attend_back(
    tiles, heads, grad, weight, query, key, value, logsum, cos, sin, grads, grads_rel, key_grad, value_grad
):
    length = query.shape[0]
    rows = length // 4
    scale = HD**-0.5
    for tile in tiles:
        at, seen = slice(tile * rows, (tile + 1) * rows), (tile + 1) * rows
        to = pl.ds(pl.multiple_of(place_of(tile) * rows, rows), rows)
        grad_context = dot(grad[to, :], weight[...], 1, 1).astype(BF16)
        for head in range(heads):
            columns = slice(head * HD, (head + 1) * HD)
            head_query = query[at, columns]
            scores = masked_scores(head_query, key[:seen, :], tile * rows, scale)
            prob = jnp.exp(scores - logsum[at, head : head + 1])
            head_grad = grad_context[:, columns]
            dprob = dot(head_grad, value[:seen, :], 1, 1)
            delta = jnp.sum(prob * dprob, axis=-1, keepdims=True)
            dscore = (prob * (dprob - delta)).astype(BF16)
            dquery = dot(dscore, key[:seen, :], 1, 0) * scale
            dquery = turned(dquery, cos[at, :], sin[at, :], True).astype(BF16)
            grads[at, columns] = dquery
            grads_rel[to, columns] = dquery
            dkey = dot(dscore, head_query, 0, 0)
            dvalue = dot(prob.astype(BF16), head_grad, 0, 0)
            key_grad[:seen, :] += dkey
            value_grad[:seen, :] += dvalue


def attend_back_end(heads, cos, sin, grads, grads_rel, key_grad, value_grad):
    rows = grads.shape[0] // 4
    scale = HD**-0.5
    for tile in range(4):
        at = slice(tile * rows, (tile + 1) * rows)
        to = pl.ds(pl.multiple_of(place_of(tile) * rows, rows), rows)
        dkey = turned(key_grad[at, :] * scale, cos[at, :], sin[at, :], True).astype(BF16)
        both = jnp.concatenate([dkey, value_grad[at, :].astype(BF16)], 1)
        grads[at, heads * HD :] = both
        grads_rel[to, heads * HD :] = both


def attend_out_kernel(tensors, line, *refs):
    refs = list(refs)
    ins_there, stream = [refs.pop(0) for _ in range(3)], refs.pop(0)
    arrived = refs.pop(0) if line else None
    outs_there = [refs.pop(0) for _ in range(3)]
    second = refs.pop(0) if line else None
    context, weight, gain = ins = [refs.pop(0) for _ in range(3)]
    own, pair, after = [refs.pop(0) for _ in range(3)]
    sent, got, crossing, crossed, stream_in, local, send, recv = refs
    copies = Copies(tensors, send, recv)
    moves = Moves(local)
    moves.start(*zip(ins_there, ins))
    position = lax.axis_index("expert") // 2
    copies.greet([copies.core, copies.far, copies.mate], line)
    rows = after.shape[0]
    quarter = pl.ds(pl.multiple_of(lax.axis_index("tensor") * rows, rows), rows)
    moves.start((stream.at[quarter], stream_in))
    if line:
        inner = (position > 0) & (position < line - 1)
        up = copies.along(arrived.at[1], second, 1, inner, position >= line // 2)
        down = copies.along(arrived.at[0], second, -1, inner, position < line // 2)

    def part(place):
        return dot(context[place * rows : (place + 1) * rows, :], weight[...], 1, 0)

    moves.wait()
    total = sum_quarter(copies, part, sent, got, crossing, crossed)
    total = stream_in[...].astype(F32) + total
    after[...] = total
    own[:rows, :] = rms_norm(total, gain[...])[0].astype(BF16)
    mate = copies.start(own.at[pl.ds(0, rows)], pair.at[pl.ds(0, rows)], copies.mate)
    moves.start((after, outs_there[2]))
    gather_quarters(copies, own, rows)
    mate.wait_recv()
    moves.start((own, outs_there[0]))
    if line:
        moves.start((pair, outs_there[1]))
        up.wait_recv()
        down.wait_recv()
    else:
        gather_quarters(copies, pair, rows)
        moves.start((pair, outs_there[1]))
    moves.wait()
    copies.finish()


def in_hbm(dims, dtype):
    return pltpu.HBM(dims, dtype)


def in_place(operands):
    return [pltpu.with_memory_space_constraint(o, pltpu.HBM) if o.size >= 2**16 else o for o in operands]


def vmem():
    return pl.BlockSpec(memory_space=pltpu.VMEM)


def attend_out(tensors, line, context, weight, gain, stream, arrived):
    length, width = stream.shape
    rows = length // 4
    outs = [((length, width), BF16), ((rows if line else length, width), BF16), ((rows, width), F32)]
    operands = in_place([context, weight, gain])
    stream, *arrived = in_place([stream] + ([arrived] if line else []))
    return pl.pallas_call(
        functools.partial(attend_out_kernel, tensors, line),
        out_shape=[in_hbm(*out) for out in outs]
        + ([in_hbm(arrived[0].shape[1:], BF16)] if line else []),
        in_specs=[anywhere()] * (4 + bool(line)),
        out_specs=[anywhere()] * (3 + bool(line)),
        scratch_shapes=buffers_of(operands)
        + [pltpu.VMEM(*out) for out in outs]
        + [
            pltpu.VMEM((2 * rows, width), BF16),
            pltpu.VMEM((2 * rows, width), BF16),
            pltpu.VMEM((rows, width), BF16),
            pltpu.VMEM((rows, width), BF16),
            pltpu.VMEM((rows, width), BF16),
            pltpu.SemaphoreType.DMA((7,)),
            pltpu.SemaphoreType.DMA((12,)),
            pltpu.SemaphoreType.DMA((12,)),
        ],
        compiler_params=pltpu.CompilerParams(
            collective_id=1, has_side_effects=True, vmem_limit_bytes=40 * 2**20
        ),
        cost_estimate=pl.CostEstimate(flops=6 * 10**10, bytes_accessed=10**7, transcendentals=0),
    )(*operands, stream, *arrived)


def hidden_units(weight, tile, grad_tile, gate, hidden):
    pre = dot(weight[: 2 * hidden, :], tile, 1, 1)
    back = dot(weight[2 * hidden :, :], grad_tile, 1, 1)
    gate_pre, up_pre = pre[:hidden], pre[hidden:]
    sigmoid = jax.nn.sigmoid(gate_pre)
    activated = gate_pre * sigmoid
    hid = (activated * up_pre).astype(BF16).astype(F32)
    row = jnp.sum(hid * back, axis=0, keepdims=True)
    grad_hidden = back * gate
    grad_pre = jnp.concatenate(
        [
            (grad_hidden * up_pre * (sigmoid * (1.0 + gate_pre * (1.0 - sigmoid)))).astype(BF16),
            (grad_hidden * activated).astype(BF16),
        ],
        0,
    )
    return row, (hid * gate).astype(BF16), grad_pre


def slot_offset(slot, position, line):
    if slot == 0:
        return 0
    table = [row[slot - 1] for row in nearest_first(line)]
    offset = table[0]
    for place in range(1, line):
        offset = offset + (table[place] - table[place - 1]) * (position // place > 0)
    return offset


def first_pass_kernel(tensors, experts, line, hidden, *refs):
    refs = list(refs)
    router, routes_own, routes_pair = [refs.pop(0) for _ in range(3)]
    own_there, quarter, grad_own_there, grad_pair_there, arrived, second = [refs.pop(0) for _ in range(6)]
    own_weights = [refs.pop(0) for _ in range(3)]
    pair_there = refs.pop(0)
    outs_there = [[refs.pop(0) for _ in range(7)] for _ in range(2)]
    last_weight, all_down = refs.pop(0), refs.pop(0)
    pair = refs.pop(0)
    outs = [[refs.pop(0) for _ in range(7)] for _ in range(2)]
    own, grad_own, grad_pair, weights, local, stores, send, recv = refs
    copies = Copies(tensors, send, recv)
    moves = Moves(stores)
    expert = lax.axis_index("expert")
    position, side = expert // 2, expert % 2
    copies.greet([copies.core, copies.far], line)
    rows = quarter.shape[0]
    inner = (position > 0) & (position < line - 1)
    outer = jnp.logical_not(inner)
    down = copies.along(second, weights.at[3], -1, position == 1, position == 0)
    up = copies.along(second, weights.at[3], 1, position == line - 2, position == line - 1)
    far = copies.start(quarter, pair.at[pl.ds(rows, rows)], copies.far)
    first = copies.start(quarter, pair.at[pl.ds(2 * rows, rows)], copies.core)

    def load(source, target, place):
        return pltpu.make_async_copy(source, target, local.at[place])

    loads = [
        *[
            load(weight, weights.at[0, pl.ds(index * hidden, hidden)], (0, 8, 9)[index])
            for index, weight in enumerate(own_weights)
        ],
        load(own_there, own, 1),
        load(grad_own_there, grad_own, 2),
        load(arrived.at[0], weights.at[1], 3),
    ]
    for copy in loads:
        copy.start()
    pl.when(inner)(lambda: load(arrived.at[1], weights.at[2], 4).start())
    pl.when(outer)(lambda: load(second, weights.at[2], 4).start())
    later = [load(quarter, pair.at[pl.ds(0, rows)], 5), load(grad_pair_there, grad_pair, 6)]
    for copy in later:
        copy.start()
    spare = load(second, weights.at[3], 7)
    pl.when(inner)(lambda: spare.start())
    names = [(position + slot_offset(slot, position, line)) * 2 + side for slot in range(line)]
    tile = 2 * rows

    def run(tokens, grads, routes, out, which):
        total_out, gated_out, grad_pre_out, rows_out, last_gate_out, probs_out, named_out = out
        at = pl.ds(which * tile, tile)
        tokens_tile, grad_tile = tokens[at, :], grads[at, :]
        logits = dot(router[...], tokens_tile, 1, 1)[:experts]
        logit_exp = jnp.exp(logits - jnp.max(logits, axis=0, keepdims=True))
        probs = logit_exp / jnp.sum(logit_exp, axis=0, keepdims=True)
        number = lax.broadcasted_iota(jnp.int32, probs.shape, 0)
        named = jnp.zeros(probs.shape, F32)
        for choice in range(routes.shape[0] // 2):
            named = jnp.where(routes[choice : choice + 1, at] == number, 1.0, named)
        gates = probs * named
        probs_out[:, at] = probs
        named_out[:, at] = named

        def gate_of(slot):
            return jnp.sum(jnp.where(number == names[slot], gates, 0.0), axis=0, keepdims=True)

        last_gate_out[0:1, at] = gate_of(line - 1)
        total = None
        for slot in range(line - 1):
            row, gated, grad_pre = hidden_units(
                weights.at[slot], tokens_tile, grad_tile, gate_of(slot), hidden
            )
            rows_out[slot : slot + 1, at] = row
            gated_out[slot * hidden : (slot + 1) * hidden, at] = gated
            grad_pre_out[2 * slot * hidden : 2 * (slot + 1) * hidden, at] = grad_pre
            part = dot(grad_pre, weights[slot, : 2 * hidden, :], 0, 0)
            total = part if total is None else total + part
        total_out[at, :] = total.astype(BF16)

    for copy in loads:
        copy.wait()
    load(second, weights.at[2], 4).wait()
    for which in range(2):
        run(own, grad_own, routes_own, outs[0], which)
    moves.start(*zip(outs[0], outs_there[0]))
    for slot in range(line - 1):
        moves.start((weights.at[slot, pl.ds(2 * hidden, hidden)], all_down.at[pl.ds(slot * hidden, hidden)]))
    far.wait_recv()
    last = copies.start(pair.at[pl.ds(rows, rows)], pair.at[pl.ds(3 * rows, rows)], copies.core)
    for copy in later:
        copy.wait()
    run(pair, grad_pair, routes_pair, outs[1], 0)
    first.wait_recv()
    last.wait_recv()
    run(pair, grad_pair, routes_pair, outs[1], 1)
    moves.start((pair, pair_there), *zip(outs[1], outs_there[1]))
    pl.when(inner)(lambda: spare.wait())
    up.wait_recv()
    down.wait_recv()
    slot = line - 1
    moves.start((weights.at[slot, pl.ds(2 * hidden, hidden)], all_down.at[pl.ds(slot * hidden, hidden)]))
    moves.start((weights.at[slot], last_weight))
    moves.wait()
    copies.finish()


def first_pass(tensors, experts, line, hidden, *operands):
    length, width = operands[3].shape
    operands = in_place(operands)
    count = line - 1
    out = [
        ((length, width), BF16),
        ((count * hidden, length), BF16),
        ((2 * count * hidden, length), BF16),
        ((8, length), F32),
        ((8, length), F32),
        ((experts, length), F32),
        ((experts, length), F32),
    ]
    tokens = pltpu.VMEM((length, width), BF16)
    whole = [((length, width), BF16)] + out * 2
    return pl.pallas_call(
        functools.partial(first_pass_kernel, tensors, experts, line, hidden),
        out_shape=[in_hbm(*o) for o in whole]
        + [in_hbm((3 * hidden, width), BF16), in_hbm((line * hidden, width), BF16)],
        in_specs=[vmem()] * 3 + [anywhere()] * 9,
        out_specs=[anywhere()] * 17,
        scratch_shapes=[pltpu.VMEM(*o) for o in whole]
        + [
            tokens,
            tokens,
            tokens,
            pltpu.VMEM((line, 3 * hidden, width), BF16),
            pltpu.SemaphoreType.DMA((10,)),
            pltpu.SemaphoreType.DMA((20,)),
            pltpu.SemaphoreType.DMA((5,)),
            pltpu.SemaphoreType.DMA((5,)),
        ],
        compiler_params=pltpu.CompilerParams(
            collective_id=5, has_side_effects=True, vmem_limit_bytes=63 * 2**20
        ),
        cost_estimate=pl.CostEstimate(flops=5 * 10**10, bytes_accessed=10**7, transcendentals=0),
    )(*operands)


def tokens_back_kernel(tensors, line, hidden, heads, *refs):
    refs = list(refs)
    gate_rows = [refs.pop(0) for _ in range(4 if line else 1)]
    probs_all, named_all, router, gain = [refs.pop(0) for _ in range(4)]
    ins_there = [refs.pop(0) for _ in range(11)]
    attn_in, grad_there, sent_pair, sent_own = [refs.pop(0) for _ in range(4)]
    factors = [refs.pop(0) for _ in range(10 if line else 0)]
    all_down, last_grad = (refs.pop(0), refs.pop(0)) if line else (None, None)
    moe_own, moe_pair = (refs.pop(0), refs.pop(0)) if not line else (None, None)
    outs_there = [refs.pop(0) for _ in range(6)]
    partial_there, moe_got = refs.pop(0), refs.pop(0)
    if line:
        moe_own, moe_pair = refs.pop(0), refs.pop(0)
    weight_grads = [refs.pop(0) for _ in range(line - 1 if line else 0)]
    lines_there = [refs.pop(0) for _ in range(2 if line else 0)]
    ins, outs = [refs.pop(0) for _ in range(11)], [refs.pop(0) for _ in range(6)]
    kept_pair, kept_own, after, w_output, query, key, value, logsum, cos, sin, context = ins
    grad_after, grad_router, grad_second, grads_rel, moe_out, moe_cross = outs
    whole, attn_grads, key_grad, value_grad, kv_got = [refs.pop(0) for _ in range(5)]
    moe_half, moe_mate, grad, block, local, stores = [refs.pop(0) for _ in range(6)]
    if line:
        first_in, first_out, up_in, down_in, turning, down_in_place = [refs.pop(0) for _ in range(6)]
        going = first_in
    got_pair, got_own, crossing_pair, crossed_pair, crossing_own, crossed_own = [refs.pop(0) for _ in range(6)]
    mate_out, mate_in, rows_kept, rows_sent, rows_got = [refs.pop(0) for _ in range(5)]
    rows_crossing, rows_crossed, rows_mine, rows_mate, send, recv = refs
    copies = Copies(tensors, send, recv)
    moves = Moves(stores)
    rows = grad.shape[0]
    moves.start(*zip(ins_there, ins), (grad_there.at[pl.ds(0, rows)], grad))
    if line:
        moves.start((all_down, down_in_place))
    position = lax.axis_index("expert") // 2
    copies.greet([copies.core, copies.far, copies.mate], line)
    if line:
        for index, (first, last) in enumerate(zip(gate_rows[::2], gate_rows[1::2])):
            top, low = slice(index * line, (index + 1) * line - 1), slice((index + 1) * line - 1, (index + 1) * line)
            for half, out in enumerate((rows_kept, rows_sent)):
                columns = slice(2 * half * rows, 2 * (half + 1) * rows)
                out[top, :] = first[: line - 1, columns]
                out[low, :] = last[:, columns]
    else:
        rows_kept[...] = gate_rows[0][:, : 2 * rows]
        rows_sent[...] = gate_rows[0][:, 2 * rows :]
    probs, named = probs_all[:, :rows], named_all[:, :rows]
    moe_core = []

    def experts_out():
        if line:
            first_rows = (line - 1) * hidden

            def body(first, last, out):
                total = dot(first[...], down_in_place[:first_rows, :], 0, 0)
                out[...] = (total + dot(last[...], down_in_place[first_rows:, :], 0, 0)).astype(BF16)

            for gated, last, out in ((factors[2], factors[4], moe_own), (factors[3], factors[5], moe_pair)):
                pltpu.emit_pipeline(
                    body,
                    grid=(4,),
                    in_specs=[
                        pl.BlockSpec((first_rows, rows), lambda i: (0, i)),
                        pl.BlockSpec((hidden, rows), lambda i: (0, i)),
                    ],
                    out_specs=[pl.BlockSpec((rows, moe_own.shape[1]), lambda i: (i, 0))],
                )(gated, last, out)
        for side, source in enumerate((moe_own, moe_pair)):
            moe_core.append(
                copies.start(source.at[pl.ds(2 * rows, 2 * rows)], moe_got.at[side], copies.core)
            )

    def make_weight_grads(slots, factors, tokens):
        count = len(slots)
        length, width = tokens[0].shape
        tile = width // 6
        once = pl.Buffered(buffer_count=1)
        pre_spec = pl.BlockSpec((2 * hidden * count, length), lambda i: (0, 0), pipeline_mode=once)
        gated_spec = pl.BlockSpec((hidden * count, length), lambda i: (0, 0), pipeline_mode=once)
        token_spec = pl.BlockSpec((length, tile), lambda i: (0, i))

        def body(pre_own, pre_pair, gated_own, gated_pair, own, pair, grad_own, grad_pair, *outs):
            for index, out in enumerate(outs):
                pre = slice(2 * hidden * index, 2 * hidden * (index + 1))
                gated = slice(hidden * index, hidden * (index + 1))
                total = dot(pre_own[pre, :], own[...], 1, 0) + dot(pre_pair[pre, :], pair[...], 1, 0)
                out[: 2 * hidden, :] = total.astype(out.dtype)
                total = dot(gated_own[gated, :], grad_own[...], 1, 0)
                total = total + dot(gated_pair[gated, :], grad_pair[...], 1, 0)
                out[2 * hidden :, :] = total.astype(out.dtype)

        pltpu.emit_pipeline(
            body,
            grid=(6,),
            in_specs=[pre_spec] * 2 + [gated_spec] * 2 + [token_spec] * 4,
            out_specs=[pl.BlockSpec((3 * hidden, tile), lambda i: (0, i))] * count,
        )(*factors, *tokens, *[weight_grads[slot] for slot in slots])

    low, high = pl.ds(0, rows), pl.ds(rows, rows)
    pair_last = copies.start(sent_pair.at[high], got_pair.at[high], copies.core)
    pair_first = copies.start(sent_pair.at[low], got_pair.at[low], copies.core)
    rows_core = copies.start(rows_sent, rows_got, copies.core)
    own_last = copies.start(sent_own.at[high], got_own.at[high], copies.core)
    own_first = copies.start(sent_own.at[low], got_own.at[low], copies.core)
    if line:
        up = copies.along(last_grad, first_in, 1, position == 0, position == 1)
        down = copies.along(last_grad, first_in, -1, position == line - 1, position == line - 2)
        inner = (position > 0) & (position < line - 1)
    moves.wait()
    pair_last.wait_recv()
    crossing_pair[...] = (kept_pair[rows:, :].astype(F32) + got_pair[rows:, :].astype(F32)).astype(BF16)
    pair_far = copies.start(crossing_pair, crossed_pair, copies.far)
    rows_core.wait_recv()
    rows_crossing[...] = rows_kept[:, rows:] + rows_got[:, rows:]
    rows_far = copies.start(rows_crossing, rows_crossed, copies.far)
    pair_first.wait_recv()
    mine_pair = kept_pair[:rows, :].astype(F32) + got_pair[:rows, :].astype(F32)
    own_last.wait_recv()
    crossing_own[...] = (kept_own[rows:, :].astype(F32) + got_own[rows:, :].astype(F32)).astype(BF16)
    own_first.wait_recv()
    grad_tokens = kept_own[:rows, :].astype(F32) + got_own[:rows, :].astype(F32)
    if line:
        make_weight_grads(list(range(line - 1)), factors[:4], factors[6:])
    pair_far.wait_recv()
    own_far = copies.start(crossing_own, crossed_own, copies.far)
    mate_out[...] = (mine_pair + crossed_pair[...].astype(F32)).astype(BF16)
    mate = copies.start(mate_out, mate_in, copies.mate)
    rows_far.wait_recv()
    rows_mine[...] = rows_kept[:, :rows] + rows_got[:, :rows] + rows_crossed[...]
    rows_over = copies.start(rows_mine, rows_mate, copies.mate)
    def move(source, target, place):
        copy = pltpu.make_async_copy(source, target, local.at[place])
        copy.start()
        copy.wait()

    def moe_part(side, at):
        move((moe_own, moe_pair)[side].at[at], block.at[0], 0)
        move(moe_got.at[side, at], block.at[1], 0)
        return block[0].astype(F32) + block[1].astype(F32)

    experts_out()
    for copy in moe_core:
        copy.wait_recv()
    for place in range(2):
        moe_half[place] = moe_part(1, pl.ds(place * rows, rows)).astype(BF16)
    rows_over.wait_recv()
    count = rows_mine.shape[0] // 2
    slots = jnp.concatenate([rows_mine[:count, :], rows_mate[count:, :]], 0)
    dprobs = jnp.zeros(probs.shape, F32)
    number = lax.broadcasted_iota(jnp.int32, probs.shape, 0)
    chip_side = lax.axis_index("expert") % 2
    for slot in range(count):
        at = position + slot_offset(slot, position, line) if line else slot
        for half in range(2):
            name = at * 2 + chip_side + half - 2 * half * chip_side
            row = slots[half * count + slot : half * count + slot + 1, :]
            dprobs = jnp.where(number == name, row, dprobs)
    dprobs = dprobs * named
    dlogits = (
        probs * (dprobs - jnp.sum(probs * dprobs, axis=0, keepdims=True))
    ).astype(BF16)
    second_out, normed, inverse = rms_norm(after[...], gain[...])
    grad_router[...] = dot(dlogits, second_out.astype(BF16), 1, 0)
    grad_tokens = grad_tokens + dot(dlogits, router[...], 0, 0)
    own_far.wait_recv()
    grad_tokens = grad_tokens + crossed_own[...].astype(F32)
    mate.wait_recv()
    moe_over = copies.start(moe_half, moe_mate, copies.mate)
    grad_tokens = grad_tokens + mate_in[...].astype(F32)
    through, second = norm_backward(grad_tokens, normed, inverse, gain[...])
    grad_second[...] = second[None]
    total = grad[...].astype(F32) + through
    grad_after[...] = total
    whole[:rows, :] = total.astype(BF16)
    moves.start(*zip(outs[:3], outs_there[:3]))
    moves.start((attn_in.at[pl.ds(0, 2 * rows)], got_pair), (attn_in.at[pl.ds(2 * rows, 2 * rows)], got_own))
    second = []

    def second_round():
        up.wait_recv()
        down.wait_recv()

        @pl.when(inner)
        def _():
            move(last_grad, first_out, 0)
            first_out[...] = (first_out[...].astype(F32) + first_in[...].astype(F32)).astype(BF16)

        @pl.when(jnp.logical_not(inner))
        def _():
            move(weight_grads[line - 2], first_out, 0)

        second.append(copies.along(first_out, up_in, 1, position < line // 2, inner))
        second.append(copies.along(first_out, down_in, -1, position >= line // 2, inner))

    def beside():
        if line:
            second_round()
        moe_cross[...] = moe_part(0, pl.ds(rows, rows)).astype(BF16)
        moe_out[...] = after[...] + moe_part(0, pl.ds(0, rows))

    far = copies.start(whole.at[pl.ds(0, rows)], whole.at[pl.ds(rows, rows)], copies.far)
    first = copies.start(whole.at[pl.ds(0, rows)], whole.at[pl.ds(2 * rows, rows)], copies.core)
    beside()
    key_grad[...] = jnp.zeros(key_grad.shape, F32)
    value_grad[...] = jnp.zeros(value_grad.shape, F32)
    attention = [w_output, query, key, value, logsum, cos, sin, attn_grads, grads_rel, key_grad, value_grad]
    low_half = lax.axis_index("tensor") // 2 == 0
    high_half = lax.axis_index("tensor") // 2 > 0
    first.wait_recv()
    pl.when(low_half)(lambda: attend_back((1, 0), heads, whole, *attention))
    pl.when(high_half)(lambda: attend_back((3, 2), heads, whole, *attention))
    far.wait_recv()
    last = copies.start(whole.at[pl.ds(rows, rows)], whole.at[pl.ds(3 * rows, rows)], copies.core)
    last.wait_recv()
    pl.when(low_half)(lambda: attend_back((3, 2), heads, whole, *attention))
    pl.when(high_half)(lambda: attend_back((1, 0), heads, whole, *attention))
    attend_back_end(heads, cos, sin, attn_grads, grads_rel, key_grad, value_grad)
    moves.start((grads_rel, outs_there[3]))

    lead = lax.axis_index("tensor") % 2
    query_width = heads * HD
    first_rows = partial_there.shape[0] // 8
    kept_at = pl.ds(pl.multiple_of(query_width + lead * HD, HD), HD)
    sent_at = pl.ds(pl.multiple_of(query_width + (1 - lead) * HD, HD), HD)
    width = whole.shape[1]
    moves.wait()

    def by_columns(columns, grads_at):
        total = dot(got_pair[:, columns], attn_grads[: 2 * rows, grads_at], 0, 0)
        return total + dot(got_own[:, columns], attn_grads[2 * rows :, grads_at], 0, 0)

    copies.drain(pair_far)
    for block_at in range(0, width, HD):
        columns = slice(block_at, block_at + HD)
        crossing_pair[:HD, columns] = by_columns(columns, sent_at).astype(BF16)
    kv = copies.start(crossing_pair.at[pl.ds(0, HD)], kv_got, copies.core)
    for block_at in range(0, width, query_width):
        columns = slice(block_at, block_at + query_width)
        query_block = by_columns(columns, slice(0, query_width)).astype(BF16)
        kept_pair[:first_rows, columns] = query_block[:first_rows]
        kept_pair[first_rows + HD : query_width + HD, columns] = query_block[first_rows:]
    kept_own[:query_width, :] = dot(context[...], whole[...], 0, 0).astype(BF16)
    kv.wait_recv()
    for block_at in range(0, width, HD):
        columns = slice(block_at, block_at + HD)
        kept = by_columns(columns, kept_at)
        kept_pair[first_rows : first_rows + HD, columns] = (kept + kv_got[:, columns].astype(F32)).astype(BF16)
    top = query_width + HD
    moves.start(
        (kept_pair.at[pl.ds(0, top)], partial_there.at[pl.ds(0, top)]),
        (kept_own.at[pl.ds(0, query_width)], partial_there.at[pl.ds(top, query_width)]),
    )
    moe_over.wait_recv()
    moe_out[...] += moe_mate[0].astype(F32)
    moe_cross[...] = (moe_cross[...].astype(F32) + moe_mate[1].astype(F32)).astype(BF16)
    moves.start(*zip(outs[4:], outs_there[4:]))
    if line:
        move(weight_grads[1], going, 0)
        move(weight_grads[2], turning, 0)
        for copy in second:
            copy.wait_recv()

        @pl.when(inner)
        def _():
            going[...] = (going[...].astype(F32) + up_in[...].astype(F32)).astype(BF16)
            turning[...] = (turning[...].astype(F32) + down_in[...].astype(F32)).astype(BF16)

        moves.start((going, lines_there[0]), (turning, lines_there[1]))
    moves.wait()
    copies.finish()


def tokens_back(tensors, experts, line, hidden, heads, length, width, *operands):
    rows = length // 4
    half = ((2 * rows, width), BF16)
    quarter = ((rows, width), BF16)
    shard = ((3 * hidden, width), BF16)
    small = ((experts, rows), F32)
    both = ((experts, 2 * rows), F32)
    outs = [
        ((rows, width), F32),
        ((experts, width), F32),
        ((1, width), F32),
        ((length, (heads + 2) * HD), BF16),
        ((rows, width), F32),
        quarter,
    ]
    there = [((2 * heads * HD + HD, width), BF16), ((2, 2 * rows, width), BF16)]
    if line:
        there += [((length, width), BF16)] * 2 + [((3 * hidden, width), F32)] + [shard] * (line - 2) + [shard] * 2
    first = 8 if line else 5
    scratch = outs + [
        ((length, width), BF16),
        ((length, (heads + 2) * HD), BF16),
        ((length, HD), F32),
        ((length, HD), F32),
        ((HD, width), BF16),
        ((2, rows, width), BF16),
        ((2, rows, width), BF16),
        quarter,
        ((2, rows, width), BF16),
    ]
    later = [half, half] + [quarter] * 6 + [both, both, both] + [small] * 4
    if line:
        later = [shard] * 5 + [((line * hidden, width), BF16)] + later
    operands = in_place(operands)
    return pl.pallas_call(
        functools.partial(tokens_back_kernel, tensors, line, hidden, heads),
        out_shape=[in_hbm(*o) for o in outs + there],
        in_specs=[vmem()] * first + [anywhere()] * (len(operands) - first),
        out_specs=[anywhere()] * len(outs + there),
        scratch_shapes=buffers_of(operands[first : first + 11])
        + [pltpu.VMEM(*o) for o in scratch]
        + [pltpu.SemaphoreType.DMA((1,)), pltpu.SemaphoreType.DMA((32,))]
        + [pltpu.VMEM(*o) for o in later]
        + [pltpu.SemaphoreType.DMA((24,)), pltpu.SemaphoreType.DMA((24,))],
        compiler_params=pltpu.CompilerParams(
            collective_id=2, has_side_effects=True, vmem_limit_bytes=63 * 2**20
        ),
        cost_estimate=pl.CostEstimate(flops=10**11, bytes_accessed=10**7, transcendentals=0),
    )(*operands)


def line_sum(copies, line, partial_there, partial, whole, got, running, up_in, down_in):
    position, side = lax.axis_index("expert") // 2, lax.axis_index("expert") % 2
    count = partial.shape[0] // 2
    chunk = count // line
    order = [3 * (1 - position // 2), 2 - position // 2, position + 1 - 2 * (position % 2), position]
    over = []

    def rows_at(half, place):
        return pl.ds(pl.multiple_of(half * count + place * chunk, 16), chunk)

    def send_pair():
        for place in order:
            over.append(
                copies.start(partial_there.at[rows_at(1 - side, place)], got.at[rows_at(0, place)], copies.mate)
            )

    def part(place):
        mine = partial[rows_at(side, place), :].astype(F32)
        return mine + got[rows_at(0, place), :].astype(F32)

    flows = {1: {}, -1: {}}

    def reach_step(reach):
        over[line - 1 - reach].wait_recv()
        for way, (step, landed) in enumerate(((1, up_in), (-1, down_in))):
            target = position + step * reach
            sends = (target >= 0) & (target < line)
            origin = position - step
            receives = (origin >= 0) & (origin < line) & (origin + step * reach >= 0) & (origin + step * reach < line)
            slot = 3 * way + reach - 1
            if reach < line - 1:
                flows[step][reach + 1].wait_recv()

            @pl.when(sends)
            def _(slot=slot, target=target, landed=landed, step=step):
                running[slot] = part(target).astype(BF16)
                if reach < line - 1:

                    @pl.when((position - step >= 0) & (position - step < line))
                    def _():
                        total = part(target) + landed[reach].astype(F32)
                        running[slot] = total.astype(BF16)

            flows[step][reach] = copies.along(running.at[slot], landed.at[reach - 1], step, sends, receives)

    spread, mates = {}, {}

    def settle():
        over[line - 1].wait_recv()
        flows[1][1].wait_recv()
        flows[-1][1].wait_recv()
        total = part(position)
        total = total + jnp.where(position > 0, up_in[0].astype(F32), 0.0)
        total = total + jnp.where(position < line - 1, down_in[0].astype(F32), 0.0)
        here = rows_at(side, position)
        whole[here, :] = total.astype(BF16)
        mates[0] = [copies.start(whole.at[here], whole.at[here], copies.mate)]

    def spread_start(hop):
        spread[hop] = []
        for step in (1, -1):
            place = position - step * (hop - 1)
            sends = (place >= 0) & (place < line) & (position + step >= 0) & (position + step < line)
            origin = position - step * hop
            receives = (origin >= 0) & (origin < line)
            at = rows_at(side, jnp.clip(place, 0, line - 1))
            spread[hop].append(copies.along(whole.at[at], whole.at[at], step, sends, receives))

    def spread_end(hop):
        mates[hop] = []
        for step, copy in zip((1, -1), spread[hop]):
            copy.wait_recv()
            origin = position - step * hop
            there = (origin >= 0) & (origin < line)
            at = rows_at(side, jnp.clip(origin, 0, line - 1))
            mates[hop].append(copies.over_when(whole.at[at], whole.at[at], copies.mate, there))

    def mates_end(hop):
        for copy in mates[hop]:
            copy.wait_recv()

    return send_pair, reach_step, settle, spread_start, spread_end, mates_end


class SmallSum:
    def __init__(self, copies, devices, running, arrived, sums):
        self.copies, self.devices, self.running, self.arrived, self.sums = copies, devices, running, arrived, sums
        self.at, self.copy = 0, None

    def step(self):
        if self.copy is not None:
            self.copy.wait_recv()
            total = self.running[self.at] + self.arrived[self.at]
            self.at += 1
            self.copy = None
            if self.at == len(self.devices):
                self.sums[...] = total
            else:
                self.running[self.at] = total
        if self.at < len(self.devices):
            self.copy = self.copies.start(
                self.running.at[self.at], self.arrived.at[self.at], self.devices[self.at]
            )

    def end(self):
        while self.copy is not None:
            self.step()


class Gather:
    def __init__(self, copies, tensors, whole, rows):
        self.copies, self.whole, self.rows = copies, whole, rows
        tensor = lax.axis_index("tensor")
        self.mine = pl.ds(pl.multiple_of(tensor * rows, rows), rows)
        self.there = pl.ds(pl.multiple_of((tensor + tensors // 2) % tensors * rows, rows), rows)

    def start(self):
        self.far = self.copies.start(self.whole.at[self.mine], self.whole.at[self.mine], self.copies.far)
        self.first = self.copies.start(self.whole.at[self.mine], self.whole.at[self.mine], self.copies.core)

    def forward(self):
        self.far.wait_recv()
        self.last = self.copies.start(self.whole.at[self.there], self.whole.at[self.there], self.copies.core)

    def end(self):
        self.first.wait_recv()
        self.last.wait_recv()


def inputs_back_kernel(tensors, experts, line, hidden, *refs):
    refs = list(refs)
    gain, grad_router, grad_second = [refs.pop(0) for _ in range(3)]
    ins_there = [refs.pop(0) for _ in range(7)]
    moe_cross, stream = [refs.pop(0) for _ in range(2)]
    own_sum, going, turning = [refs.pop(0) for _ in range(3)] if line else [None] * 3
    outs_there = [refs.pop(0) for _ in range(8 if line else 5)]
    ins, outs = [refs.pop(0) for _ in range(7)], [refs.pop(0) for _ in range(8 if line else 5)]
    grads_rel, w_query, w_key, w_value, grad_after, layer_part, partial = ins
    (whole, layer, sums, summed, kv_out), weight_outs = outs[:5], outs[5:]
    moe_crossed, stream_in, local, stores = [refs.pop(0) for _ in range(4)]
    buffers = [refs.pop(0) for _ in range(4)] if line else []
    final, block = (refs.pop(0), refs.pop(0)) if line else (None, None)
    sent, got, crossing, crossed, running, arrived, send, recv = refs
    copies = Copies(tensors, send, recv)
    moves = Moves(stores)
    rows = grad_after.shape[0]
    quarter = pl.ds(pl.multiple_of(lax.axis_index("tensor") * rows, rows), rows)
    moves.start(*zip(ins_there, ins), (stream.at[quarter], stream_in))
    bits = [1 << k for k in range(experts.bit_length() - 1)]
    position = lax.axis_index("expert") // 2
    copies.greet([copies.core, copies.far] + [copies.across(bit) for bit in bits], line)
    lines = []
    moe_far = copies.start(moe_cross, moe_crossed, copies.far)
    if line:
        send_pair, reach_step, settle, spread_start, spread_end, mates_end = line_sum(
            copies, line, ins_there[6], partial, summed, *buffers
        )
        send_pair()
        end, inner = position == line - 1, (position > 0) & (position < line - 1)
        lines = [
            copies.along(going, final.at[0], 1, position < line - 1, position > 0),
            copies.along(going, final.at[1], -1, end, position == line - 2),
            copies.along(turning, final.at[1], -1, inner, position < line - 2),
        ]
    heads = w_query.shape[1] // HD
    query_width = heads * HD
    kv_rows = pl.ds(partial.shape[0] // 8, HD)
    kv_at = kv_columns(heads)
    moves.wait()

    def part(place):
        at = slice(place * rows, (place + 1) * rows)
        total = dot(grads_rel[at, :query_width], w_query[...], 1, 1)
        total = total + dot(grads_rel[at, query_width : query_width + HD], w_key[:, kv_at], 1, 1)
        return total + dot(grads_rel[at, query_width + HD :], w_value[:, kv_at], 1, 1)

    def beside():
        if line:
            reach_step(line - 1)
            reach_step(line - 2)

    grad_in = sum_quarter(copies, part, sent, got, crossing, crossed, beside)
    _, normed, inverse = rms_norm(stream_in[...].astype(F32), gain[...])
    through, first = norm_backward(grad_in, normed, inverse, gain[...])
    whole[quarter, :] = (grad_after[...] + through).astype(BF16)
    inputs_gather = Gather(copies, tensors, whole, rows)
    inputs_gather.start()
    running[0] = jnp.zeros(sums.shape, F32)
    running[0, :experts, :] = grad_router[...]
    running[0, experts : experts + 1, :] = grad_second[...]
    running[0, experts + 1 : experts + 2, :] = first[None]
    small = SmallSum(
        copies, [copies.core] + [copies.across(bit) for bit in bits] + [copies.far], running, arrived, sums
    )
    small.step()
    if line:
        for reach in range(line - 3, 0, -1):
            reach_step(reach)
    small.step()
    moe_far.wait_recv()
    layer[quarter, :] = (layer_part[...] + moe_crossed[...].astype(F32)).astype(BF16)
    layer_gather = Gather(copies, tensors, layer, rows)
    layer_gather.start()
    if line:
        settle()
        spread_start(1)
        small.step()
        spread_end(1)
        spread_start(2)
        small.step()
    inputs_gather.forward()
    if line:
        spread_end(2)
        spread_start(3)
        small.step()
        for copy in lines:
            copy.wait_recv()
        for index, out in enumerate(weight_outs):
            at = pl.ds(index * hidden, hidden)
            move = pltpu.make_async_copy(own_sum.at[at], block, local.at[0])
            move.start()
            move.wait()
            total = block[...] + jnp.where(position > 0, final[0, at, :].astype(F32), 0.0)
            total = total + jnp.where(position < line - 1, final[1, at, :].astype(F32), 0.0)
            out[...] = total
            moves.start((out, outs_there[5 + index]))
        for hop in range(3):
            mates_end(hop)
        far = copies.start(summed.at[kv_rows], kv_out.at[0], copies.far)
        near = copies.start(summed.at[kv_rows], kv_out.at[1], copies.core)
        spread_end(3)
        layer_gather.forward()
        far.wait_recv()
        across = copies.start(kv_out.at[0], kv_out.at[2], copies.core)
        mates_end(3)
        near.wait_recv()
        across.wait_recv()
    else:
        layer_gather.forward()
        summed[...] = partial[...]
        kv_out[...] = jnp.zeros(kv_out.shape, BF16)
    small.end()
    moves.start((sums, outs_there[2]), (summed, outs_there[3]), (kv_out, outs_there[4]))
    inputs_gather.end()
    layer_gather.end()
    moves.start((whole, outs_there[0]), (layer, outs_there[1]))
    moves.wait()
    copies.finish()


def inputs_back(tensors, experts, line, hidden, heads, length, width, *operands):
    rows = length // 4
    early = (-(-(experts + 2) // 8) * 8, width)
    steps = 1 + experts.bit_length()
    projected = 2 * heads * HD + HD
    quarter, half = ((rows, width), BF16), ((2 * rows, width), BF16)
    outs = [
        ((length, width), BF16),
        ((length, width), BF16),
        (early, F32),
        ((projected, width), BF16),
        ((3, HD, width), BF16),
    ]
    buffers = []
    if line:
        chunk = projected // 2 // line
        buffers = [
            ((projected // 2, width), BF16),
            ((6, chunk, width), BF16),
            ((3, chunk, width), BF16),
            ((3, chunk, width), BF16),
            ((2, 3 * hidden, width), BF16),
            ((hidden, width), F32),
        ]
        outs = outs + [((hidden, width), F32)] * 3
    buffers += [half, half, quarter, quarter, ((steps,) + early, F32), ((steps,) + early, F32)]
    operands = in_place(operands)
    return pl.pallas_call(
        functools.partial(inputs_back_kernel, tensors, experts, line, hidden),
        out_shape=[in_hbm(*o) for o in outs],
        in_specs=[vmem()] * 3 + [anywhere()] * (len(operands) - 3),
        out_specs=[anywhere()] * len(outs),
        scratch_shapes=buffers_of(operands[3:10])
        + [pltpu.VMEM(*o) for o in outs + [quarter] * 2]
        + [pltpu.SemaphoreType.DMA((1,)), pltpu.SemaphoreType.DMA((16,))]
        + [pltpu.VMEM(*o) for o in buffers]
        + [pltpu.SemaphoreType.DMA((50 + steps,)), pltpu.SemaphoreType.DMA((50 + steps,))],
        compiler_params=pltpu.CompilerParams(
            collective_id=3, has_side_effects=True, vmem_limit_bytes=63 * 2**20
        ),
        cost_estimate=pl.CostEstimate(flops=10**11, bytes_accessed=10**7, transcendentals=0),
    )(*operands)


def results_kernel(query_width, layer, inputs, gate, up, down, summed, kv_rest, *outs):
    layer_out, inputs_out, gate_out, up_out, down_out, query_out, output_out, key_out, value_out = outs
    step = pl.program_id(0)
    for source, out in ((layer, layer_out), (inputs, inputs_out), (gate, gate_out), (up, up_out), (down, down_out)):
        out[...] = source[...]
    first_rows, top = summed.shape[0] // 8, query_width + HD
    columns = pl.ds(pl.multiple_of(step * query_width, HD), query_width)
    query_out[:first_rows, :] = summed[:first_rows, columns].astype(F32)
    query_out[first_rows:, :] = summed[first_rows + HD : top, columns].astype(F32)
    part = query_width // 4
    output_out[...] = summed[pl.ds(pl.multiple_of(top + step * part, 16), part), :].astype(F32)
    tensor = lax.axis_index("tensor")
    lead, low_head = tensor % 2 == 0, tensor * (query_width // HD) // (HEADS // KV) == 0
    for block in range(query_width // HD):
        at = pl.ds(pl.multiple_of(step * query_width + block * HD, HD), HD)
        mine = summed[first_rows : first_rows + HD, at].astype(F32)
        far, core, across = [kv_rest[k, :, at].astype(F32) for k in range(3)]
        rows = slice(block * HD, (block + 1) * HD)
        for out, near, other in (
            (key_out, jnp.where(lead, mine, core), jnp.where(lead, far, across)),
            (value_out, jnp.where(lead, core, mine), jnp.where(lead, across, far)),
        ):
            out[rows, :HD] = jnp.where(low_head, near, other)
            out[rows, HD:] = jnp.where(low_head, other, near)


def results(query_width, *operands):
    (length, width), (hidden, _) = operands[0].shape, operands[2].shape
    shape = jax.ShapeDtypeStruct

    def rows(count):
        return pl.BlockSpec((count // 4, width), lambda i: (i, 0))

    def whole(dims):
        return pl.BlockSpec(dims, lambda i: (0,) * len(dims))

    def columns(count):
        return pl.BlockSpec((width // 4, count), lambda i: (i, 0))

    same = [rows(length), rows(length)] + [rows(hidden)] * 3
    return pl.pallas_call(
        functools.partial(results_kernel, query_width),
        grid=(4,),
        in_specs=same + [whole(operands[5].shape), whole(operands[6].shape)],
        out_specs=same + [columns(query_width), rows(query_width), columns(2 * HD), columns(2 * HD)],
        out_shape=[shape((length, width), BF16)] * 2
        + [shape((hidden, width), F32)] * 3
        + [shape((width, query_width), F32), shape((query_width, width), F32)]
        + [shape((width, 2 * HD), F32)] * 2,
        compiler_params=pltpu.CompilerParams(vmem_limit_bytes=40 * 2**20),
        cost_estimate=pl.CostEstimate(flops=0, bytes_accessed=3 * 10**7, transcendentals=0),
    )(*in_place(operands))


def shards(
    experts,
    tensors,
    inputs,
    routes,
    cotangent,
    first_gain,
    second_gain,
    w_query,
    w_key,
    w_value,
    w_output,
    w_router,
    w_gate,
    w_up,
    w_down,
):
    links = Links(experts, tensors)
    line, place, side = links.line, links.place, links.side
    length, width = inputs.shape
    heads = w_query.shape[1] // HD
    hidden = w_gate.shape[2]
    group = HEADS // KV
    kv_head = links.tensor * heads // group
    scale = HD ** (-0.5)
    order = nearest_first(line)

    own_weights = [w_gate[0].T, w_up[0].T, w_down[0]]
    short = line if line == 4 else 0
    if not short:
        sides = [[2 * p + s for p in range(line)] for s in range(2)]
        weights = lax.all_gather(jnp.concatenate(own_weights, 0), "expert", axis_index_groups=sides)

    rows, half = length // 4, length // 2
    cos, sin = [jnp.asarray(table) for table in rotary_tables(length)]
    attn_in, query, key, value, context_rel, logsum, grad_rel, grad_pair, routes_own, routes_pair, *arrived = attend(
        tensors,
        short,
        inputs,
        first_gain[None],
        w_query,
        w_key,
        w_value,
        cos,
        sin,
        cotangent,
        routes.T,
        own_weights,
    )

    tokens_own, tokens_pair, after, *second = attend_out(
        tensors, short, context_rel, w_output, second_gain[None], inputs, *(arrived or [None])
    )
    router_rows = w_router.T
    if short:
        router_padded = jnp.concatenate([router_rows, router_rows], 0)
        tokens_pair, *outs, last_weight, all_down = first_pass(
            tensors,
            experts,
            line,
            hidden,
            router_padded,
            routes_own,
            routes_pair,
            tokens_own,
            tokens_pair,
            grad_rel,
            grad_pair,
            arrived[0],
            second[0],
            *own_weights,
        )
        *first_own, last_gate_own, router_probs, named = outs[:7]
        *first_pair, last_gate_pair, _, _ = outs[7:]
    else:
        names = jnp.arange(experts, dtype=jnp.int32)[:, None, None]

        def gates_of(tokens, tokens_routes):
            logits = dot(router_rows, tokens, 1, 1)
            logit_exp = jnp.exp(logits - jnp.max(logits, axis=0, keepdims=True))
            probs = logit_exp / jnp.sum(logit_exp, axis=0, keepdims=True)
            named = jnp.any(tokens_routes[None] == names, axis=1).astype(F32)
            return probs, named, probs * named

        router_probs, named, gates_own = gates_of(tokens_own, routes_own[:4])
        _, _, gates_pair = gates_of(tokens_pair, routes_pair[:4])
    both_tokens, both_grads = (tokens_own, tokens_pair), (grad_rel, grad_pair)
    if short:
        (kept_pair, sent_pair, *last_pair), (kept_own, sent_own, *last_own), last_grad = last_expert(
            hidden,
            last_weight,
            (tokens_pair, grad_pair, last_gate_pair, first_pair[0]),
            (tokens_own, grad_rel, last_gate_own, first_own[0]),
        )
        gate_rows = [first_own[3], last_own[1], first_pair[3], last_pair[1]]
    else:
        zeros = jnp.zeros((length, width), BF16)

        def step(totals, weight_at):
            weight, position = weight_at
            name = (position * 2 + side)[None]
            down = weight[2 * hidden :]
            own = expert_pass(tokens_own, grad_rel, gates_own, name, [weight], totals[0])
            pair = expert_pass(tokens_pair, grad_pair, gates_pair, name, [weight], totals[1])
            grads = weight_grad(
                0, hidden, (own[2], pair[2]), (own[1], pair[1]), both_tokens, both_grads, BF16
            )
            moe_own = totals[2] + dot(own[1], down, 0, 0)
            moe_pair = totals[3] + dot(pair[1], down, 0, 0)
            return (own[0], pair[0], moe_own, moe_pair), (own[3][0], pair[3][0], grads)

        (sum_own, sum_pair, moe_own, moe_pair), (gate_own, gate_pair, weight_grads) = lax.scan(
            step,
            (zeros, zeros, zeros.astype(F32), zeros.astype(F32)),
            (weights, jnp.arange(line, dtype=jnp.int32)),
        )
        kept_own, sent_own, kept_pair, sent_pair = sum_own[:half], sum_own[half:], sum_pair[:half], sum_pair[half:]

    if short:
        factors = [first_own[2], first_pair[2], first_own[1], first_pair[1]]
        factors += [last_own[0], last_pair[0], *both_tokens, *both_grads, all_down, last_grad]
    else:
        gate_rows = [jnp.concatenate([gate_own, gate_pair], 0)]
        factors = [moe_own.astype(BF16), moe_pair.astype(BF16)]
    (
        grad_after,
        grad_router,
        grad_second,
        grads_rel,
        layer_part,
        moe_cross,
        partial,
        _,
        *weight_sums,
    ) = tokens_back(
        tensors,
        experts,
        short,
        hidden,
        heads,
        length,
        width,
        *gate_rows,
        router_probs,
        named,
        router_rows,
        second_gain[None],
        kept_pair,
        kept_own,
        after,
        w_output,
        query,
        key,
        value,
        logsum,
        cos,
        sin,
        context_rel,
        attn_in,
        grad_rel,
        sent_pair,
        sent_own,
        *factors,
    )

    line_sums = []
    if short:
        line_sums = [weight_sums[2], *weight_sums[-2:]]
    else:
        expert_grads = lax.psum_scatter(
            weight_grads, "expert", scatter_dimension=0, axis_index_groups=sides
        ).astype(F32)

    grad_inputs, layer_out, sums, summed, kv_rest, *weight_grads_out = inputs_back(
        tensors,
        experts,
        short,
        hidden,
        heads,
        length,
        width,
        first_gain[None],
        grad_router,
        grad_second,
        grads_rel,
        w_query,
        w_key,
        w_value,
        grad_after,
        layer_part,
        partial,
        moe_cross,
        inputs,
        *line_sums,
    )
    query_width = heads * HD
    if not short:
        summed = lax.psum(summed, "expert")
        first_rows = summed.shape[0] // 8
        kv_far = links.over_tensor(summed[first_rows : first_rows + HD], 2)
        both = jnp.concatenate([summed[first_rows : first_rows + HD], kv_far], 0)
        kv_core = links.over_tensor(both, 1)
        kv_rest = jnp.stack([kv_far, kv_core[:HD], kv_core[HD:]])
        weight_grads_out = [expert_grads[i * hidden : (i + 1) * hidden] for i in range(3)]
    (
        layer_out,
        grad_inputs,
        grad_gate,
        grad_up,
        grad_down,
        grad_query,
        grad_output,
        grad_key,
        grad_value,
    ) = results(query_width, layer_out, grad_inputs, *weight_grads_out, summed, kv_rest)
    grad_router, grad_second, grad_first = sums[:experts].T, sums[experts], sums[experts + 1]
    return (
        layer_out,
        grad_inputs,
        grad_first,
        grad_second,
        grad_query,
        grad_key,
        grad_value,
        grad_output,
        grad_router,
        grad_gate.T[None],
        grad_up.T[None],
        grad_down[None],
    )


def solution(mesh):
    experts, tensors = mesh.shape["expert"], mesh.shape["tensor"]
    in_specs = (
        P("expert", None),
        P("expert", None),
        P("expert", None),
        P(),
        P(),
        P(None, "tensor"),
        P(),
        P(),
        P("tensor", None),
        P(),
        P("expert", None, "tensor"),
        P("expert", None, "tensor"),
        P("expert", "tensor", None),
    )
    out_specs = (
        P("expert", None),
        P("expert", None),
        P(),
        P(),
        P(None, "tensor"),
        P(),
        P(),
        P("tensor", None),
        P(),
        P("expert", None, "tensor"),
        P("expert", None, "tensor"),
        P("expert", "tensor", None),
    )

    def run(*arrays):
        return shards(experts, tensors, *arrays)

    return jax.shard_map(run, mesh=mesh, in_specs=in_specs, out_specs=out_specs, check_vma=False)
```

profile of v0, /device:TPU:1, one launch (start us, length us, event | category | flops | bytes accessed | tf_op | source)
XLA Modules:
  0.0 394.9 jit_solution(1153426342583768713)
XLA Ops:
  0.6 0.7 broadcast_in_dim.17.refs_1_.refs_0_
  1.3 0.0 copy-start
  1.3 0.7 broadcast_in_dim.18.refs_2_.refs_7_
  2.1 0.0 copy-start.1
  2.1 1.4 pad_maximum_fusion.refs_0_
  3.5 0.0 copy-start.2
  3.5 0.7 copy-done.2
  4.2 45.6 %shard_map.238 = (bf16[1024,1536]{1,0:T(8,128)(2,1)}, bf16[1024,384]{1,0:T(8,128)(2,1)}, bf16[1024,128]{1,0:T(8,128)(2,1)}, bf16[1024,128]{1,0:T(8,128)(2,1)}, b...) custom-call(bf16[1024,1536]{1,0:T(8,128)(2,1)} %refs_11_.3, ...), custom_call_target="tpu_custom_call" | custom-call | flops 40000000000 | bytes 10000000 | tf_op jit(solution)/shard_map/pallas_call | solution.py:539
  49.8 0.0 copy-done
  49.8 0.0 copy-done.1
  49.8 54.6 %shard_map.239 = (bf16[1024,1536]{1,0:T(8,128)(2,1)}, bf16[256,1536]{1,0:T(8,128)(2,1)}, f32[256,1536]{1,0:T(8,128)}, bf16[576,1536]{1,0:T(8,128)(2,1)}) custom-call(bf16[1024,384]{1,0:T(8,128)(2,1)} %get-tuple-element.80.refs_0_.refs_18_, bf16[384,1536]{1,0:T(8,128)(2,1)} %refs_11_.2, f32[1,1536]{1,0:T(1,128)S(1)} %broadcast_in_dim.18.refs_2_.refs_7_, ...), custom_call_target="tpu_custom_call" | custom-call | flops 60000002048 | bytes 10000000 | tf_op jit(solution)/shard_map/pallas_call | solution.py:664
  104.4 43.7 %shard_map.240 = (bf16[1024,1536]{1,0:T(8,128)(2,1)}, bf16[1024,1536]{1,0:T(8,128)(2,1)}, bf16[576,1024]{1,0:T(8,128)(2,1)}, bf16[1152,1024]{1,0:T(8,128)(2,1)},...) custom-call(bf16[16,1536]{1,0:T(8,128)(2,1)} %pad_maximum_fusion.ref, ...), custom_call_target="tpu_custom_call" | custom-call | flops 49999998976 | bytes 10000000 | tf_op jit(solution)/shard_map/pallas_call | solution.py:839
  148.1 23.2 %shard_map.241 = (bf16[512,1536]{1,0:T(8,128)(2,1)}, bf16[512,1536]{1,0:T(8,128)(2,1)}, bf16[192,1024]{1,0:T(8,128)(2,1)}, f32[1,1024]{1,0:T(1,128)}, bf16[512,1...) custom-call(bf16[576,1536]{1,0:T(8,128)(2,1)} %get-tuple-element.88., ...), custom_call_target="tpu_custom_call" | custom-call | flops 9663676416 | bytes 26935296 | tf_op jit(solution)/shard_map/pallas_call | solution.py:234
  171.3 95.6 %shard_map.242 = (f32[256,1536]{1,0:T(8,128)}, f32[8,1536]{1,0:T(8,128)}, f32[1,1536]{1,0:T(1,128)}, bf16[1024,640]{1,0:T(8,128)(2,1)}, f32[256,1536]{1,0:T(8,12...) custom-call(f32[8,1024]{1,0:T(8,128)} %get-tuple-element.87.refs_0_,, ...), custom_call_target="tpu_custom_call" | custom-call | flops 99999997952 | bytes 10000000 | tf_op jit(solution)/shard_map/pallas_call | solution.py:1167
  266.9 113.0 %shard_map.243 = (bf16[1024,1536]{1,0:T(8,128)(2,1)}, bf16[1024,1536]{1,0:T(8,128)(2,1)}, f32[16,1536]{1,0:T(8,128)}, bf16[896,1536]{1,0:T(8,128)(2,1)}, bf16[3,...) custom-call(f32[1,1536]{1,0:T(1,128)} %copy-done, ...), custom_call_target="tpu_custom_call" | custom-call | flops 99999997952 | bytes 10000000 | tf_op jit(solution)/shard_map/pallas_call | solution.py:1461
  379.9 1.5 slice_reduce_fusion
  381.4 1.4 slice_bitcast_fusion
  382.8 11.9 %shard_map.244 = (bf16[1024,1536]{1,0:T(8,128)(2,1)}, bf16[1024,1536]{1,0:T(8,128)(2,1)}, f32[192,1536]{1,0:T(8,128)}, f32[192,1536]{1,0:T(8,128)}, f32[192,1536...) custom-call(bf16[1024,1536]{1,0:T(8,128)(2,1)} %get-tuple-element.127.lay, ...), custom_call_target="tpu_custom_call" | custom-call | bytes 30000000 | tf_op jit(solution)/shard_map/pallas_call | solution.py:1518
Async XLA Ops:
  1.3 48.5 %copy-start = (f32[1,1536]{1,0:T(1,128)}, f32[1,1536]{1,0:T(1,128)S(1)}, u32[]{:S(2)}) copy-start(f32[1,1536]{1,0:T(1,128)S(1)} %broadcast_in_dim.17.refs_1_.refs_0_) | copy-start | bytes 18436
  2.1 47.8 %copy-start.1 = (f32[1,1536]{1,0:T(1,128)}, f32[1,1536]{1,0:T(1,128)S(1)}, u32[]{:S(2)}) copy-start(f32[1,1536]{1,0:T(1,128)S(1)} %broadcast_in_dim.18.refs_2_.refs_7_) | copy-start | bytes 18436
  3.5 0.7 copy-start.2
where the time goes:
time: 399 us; the launch traced here: 395 us
  Pallas kernels  387 us (97%)
  local copies, waits for them, and re-layouts  5.06 us (1%)
    pallas_call x1, Pallas kernels, inputs_back(): pl.pallas_call(functools.partial(inputs_back_kernel, tensors, experts, li...  113 us
    pallas_call x1, Pallas kernels, tokens_back(): pl.pallas_call(functools.partial(tokens_back_kernel, tensors, line, hidde...  95.6 us
    pallas_call x1, Pallas kernels, attend_out(): pl.pallas_call(functools.partial(attend_out_kernel, tensors, line), out_s...  54.6 us
    pallas_call x1, Pallas kernels, attend(): pl.pallas_call(functools.partial(attend_kernel, tensors, line, heads), ou...  45.6 us
    pallas_call x1, Pallas kernels, first_pass(): pl.pallas_call(functools.partial(first_pass_kernel, tensors, experts, lin...  43.7 us
    pallas_call x1, Pallas kernels, last_expert(): pl.pallas_call(functools.partial(last_expert_kernel, hidden), grid=(4,),...  23.2 us
    pallas_call x1, Pallas kernels, results(): pl.pallas_call(functools.partial(results_kernel, query_width), grid=(4,),...  11.9 us

commit v1 on v0

--- a/solution.py
+++ b/solution.py
@@ -1022,6 +1022,26 @@
     second_out, normed, inverse = rms_norm(after[...], gain[...])
     grad_router[...] = dot(dlogits, second_out.astype(BF16), 1, 0)
     grad_tokens = grad_tokens + dot(dlogits, router[...], 0, 0)
+    rounds = []
+
+    def second_round():
+        up.wait_recv()
+        down.wait_recv()
+
+        @pl.when(inner)
+        def _():
+            move(last_grad, first_out, 0)
+            first_out[...] = (first_out[...].astype(F32) + first_in[...].astype(F32)).astype(BF16)
+
+        @pl.when(jnp.logical_not(inner))
+        def _():
+            move(weight_grads[line - 2], first_out, 0)
+
+        rounds.append(copies.along(first_out, up_in, 1, position < line // 2, inner))
+        rounds.append(copies.along(first_out, down_in, -1, position >= line // 2, inner))
+
+    if line:
+        second_round()
     own_far.wait_recv()
     grad_tokens = grad_tokens + crossed_own[...].astype(F32)
     mate.wait_recv()
@@ -1034,27 +1054,8 @@
     whole[:rows, :] = total.astype(BF16)
     moves.start(*zip(outs[:3], outs_there[:3]))
     moves.start((attn_in.at[pl.ds(0, 2 * rows)], got_pair), (attn_in.at[pl.ds(2 * rows, 2 * rows)], got_own))
-    second = []
-
-    def second_round():
-        up.wait_recv()
-        down.wait_recv()
-
-        @pl.when(inner)
-        def _():
-            move(last_grad, first_out, 0)
-            first_out[...] = (first_out[...].astype(F32) + first_in[...].astype(F32)).astype(BF16)
-
-        @pl.when(jnp.logical_not(inner))
-        def _():
-            move(weight_grads[line - 2], first_out, 0)
-
-        second.append(copies.along(first_out, up_in, 1, position < line // 2, inner))
-        second.append(copies.along(first_out, down_in, -1, position >= line // 2, inner))
 
     def beside():
-        if line:
-            second_round()
         moe_cross[...] = moe_part(0, pl.ds(rows, rows)).astype(BF16)
         moe_out[...] = after[...] + moe_part(0, pl.ds(0, rows))
 
@@ -1117,7 +1118,7 @@
     if line:
         move(weight_grads[1], going, 0)
         move(weight_grads[2], turning, 0)
-        for copy in second:
+        for copy in rounds:
             copy.wait_recv()
 
         @pl.when(inner)

time: 399 us -> 406 us (1.018); the launches traced: 395 us -> 398 us
    pallas_call x1, Pallas kernels: 54.6 us -> 46 us  [attend_out(): pl.pallas_call(functools.partial(attend_out_kernel, tensors, line), out_s...]
    pallas_call x1, Pallas kernels: 43.7 us -> 51.3 us  [first_pass(): pl.pallas_call(functools.partial(first_pass_kernel, tensors, experts, lin...]
where the time goes in v1:
time: 406 us; the launch traced here: 398 us
  Pallas kernels  390 us (96%)
  local copies, waits for them, and re-layouts  5.06 us (1%)
    pallas_call x1, Pallas kernels, inputs_back(): pl.pallas_call(functools.partial(inputs_back_kernel, tensors, experts, li...  113 us
    pallas_call x1, Pallas kernels, tokens_back(): pl.pallas_call(functools.partial(tokens_back_kernel, tensors, line, hidde...  99.4 us
    pallas_call x1, Pallas kernels, first_pass(): pl.pallas_call(functools.partial(first_pass_kernel, tensors, experts, lin...  51.3 us
    pallas_call x1, Pallas kernels, attend_out(): pl.pallas_call(functools.partial(attend_out_kernel, tensors, line), out_s...  46 us
    pallas_call x1, Pallas kernels, attend(): pl.pallas_call(functools.partial(attend_kernel, tensors, line, heads), ou...  45.6 us
    pallas_call x1, Pallas kernels, last_expert(): pl.pallas_call(functools.partial(last_expert_kernel, hidden), grid=(4,),...  23.2 us
    pallas_call x1, Pallas kernels, results(): pl.pallas_call(functools.partial(results_kernel, query_width), grid=(4,),...  11.9 us

profile of v1, /device:TPU:1, one launch (start us, length us, event | category | flops | bytes accessed | tf_op | source)
XLA Modules:
  0.0 397.7 jit_solution(4752759040546672985)
XLA Ops:
  0.6 0.7 broadcast_in_dim.17.refs_1_.refs_0_
  1.3 0.0 copy-start
  1.3 0.7 broadcast_in_dim.18.refs_2_.refs_7_
  2.1 0.0 copy-start.1
  2.1 1.4 pad_maximum_fusion.refs_0_
  3.5 0.0 copy-start.2
  3.5 0.7 copy-done.2
  4.2 45.6 %shard_map.238 = (bf16[1024,1536]{1,0:T(8,128)(2,1)}, bf16[1024,384]{1,0:T(8,128)(2,1)}, bf16[1024,128]{1,0:T(8,128)(2,1)}, bf16[1024,128]{1,0:T(8,128)(2,1)}, b...) custom-call(bf16[1024,1536]{1,0:T(8,128)(2,1)} %refs_11_.3, ...), custom_call_target="tpu_custom_call" | custom-call | flops 40000000000 | bytes 10000000 | tf_op jit(solution)/shard_map/pallas_call | solution.py:539
  49.8 0.0 copy-done
  49.8 0.0 copy-done.1
  49.8 46.0 %shard_map.239 = (bf16[1024,1536]{1,0:T(8,128)(2,1)}, bf16[256,1536]{1,0:T(8,128)(2,1)}, f32[256,1536]{1,0:T(8,128)}, bf16[576,1536]{1,0:T(8,128)(2,1)}) custom-call(bf16[1024,384]{1,0:T(8,128)(2,1)} %get-tuple-element.80.refs_0_.refs_18_, bf16[384,1536]{1,0:T(8,128)(2,1)} %refs_11_.2, f32[1,1536]{1,0:T(1,128)S(1)} %broadcast_in_dim.18.refs_2_.refs_7_, ...), custom_call_target="tpu_custom_call" | custom-call | flops 60000002048 | bytes 10000000 | tf_op jit(solution)/shard_map/pallas_call | solution.py:664
  95.9 51.3 %shard_map.240 = (bf16[1024,1536]{1,0:T(8,128)(2,1)}, bf16[1024,1536]{1,0:T(8,128)(2,1)}, bf16[576,1024]{1,0:T(8,128)(2,1)}, bf16[1152,1024]{1,0:T(8,128)(2,1)},...) custom-call(bf16[16,1536]{1,0:T(8,128)(2,1)} %pad_maximum_fusion.ref, ...), custom_call_target="tpu_custom_call" | custom-call | flops 49999998976 | bytes 10000000 | tf_op jit(solution)/shard_map/pallas_call | solution.py:839
  147.2 23.2 %shard_map.241 = (bf16[512,1536]{1,0:T(8,128)(2,1)}, bf16[512,1536]{1,0:T(8,128)(2,1)}, bf16[192,1024]{1,0:T(8,128)(2,1)}, f32[1,1024]{1,0:T(1,128)}, bf16[512,1...) custom-call(bf16[576,1536]{1,0:T(8,128)(2,1)} %get-tuple-element.88., ...), custom_call_target="tpu_custom_call" | custom-call | flops 9663676416 | bytes 26935296 | tf_op jit(solution)/shard_map/pallas_call | solution.py:234
  170.4 99.4 %shard_map.242 = (f32[256,1536]{1,0:T(8,128)}, f32[8,1536]{1,0:T(8,128)}, f32[1,1536]{1,0:T(1,128)}, bf16[1024,640]{1,0:T(8,128)(2,1)}, f32[256,1536]{1,0:T(8,12...) custom-call(f32[8,1024]{1,0:T(8,128)} %get-tuple-element.87.refs_0_,, ...), custom_call_target="tpu_custom_call" | custom-call | flops 99999997952 | bytes 10000000 | tf_op jit(solution)/shard_map/pallas_call | solution.py:1168
  269.8 112.9 %shard_map.243 = (bf16[1024,1536]{1,0:T(8,128)(2,1)}, bf16[1024,1536]{1,0:T(8,128)(2,1)}, f32[16,1536]{1,0:T(8,128)}, bf16[896,1536]{1,0:T(8,128)(2,1)}, bf16[3,...) custom-call(f32[1,1536]{1,0:T(1,128)} %copy-done, ...), custom_call_target="tpu_custom_call" | custom-call | flops 99999997952 | bytes 10000000 | tf_op jit(solution)/shard_map/pallas_call | solution.py:1462
  382.7 1.5 slice_reduce_fusion
  384.2 1.4 slice_bitcast_fusion
  385.6 11.9 %shard_map.244 = (bf16[1024,1536]{1,0:T(8,128)(2,1)}, bf16[1024,1536]{1,0:T(8,128)(2,1)}, f32[192,1536]{1,0:T(8,128)}, f32[192,1536]{1,0:T(8,128)}, f32[192,1536...) custom-call(bf16[1024,1536]{1,0:T(8,128)(2,1)} %get-tuple-element.127.lay, ...), custom_call_target="tpu_custom_call" | custom-call | bytes 30000000 | tf_op jit(solution)/shard_map/pallas_call | solution.py:1519
Async XLA Ops:
  1.3 48.5 %copy-start = (f32[1,1536]{1,0:T(1,128)}, f32[1,1536]{1,0:T(1,128)S(1)}, u32[]{:S(2)}) copy-start(f32[1,1536]{1,0:T(1,128)S(1)} %broadcast_in_dim.17.refs_1_.refs_0_) | copy-start | bytes 18436
  2.1 47.8 %copy-start.1 = (f32[1,1536]{1,0:T(1,128)}, f32[1,1536]{1,0:T(1,128)S(1)}, u32[]{:S(2)}) copy-start(f32[1,1536]{1,0:T(1,128)S(1)} %broadcast_in_dim.18.refs_2_.refs_7_) | copy-start | bytes 18436
  3.5 0.7 copy-start.2
